TPU v7x, 32 devices: a whole 2x2x4 slice. The times are simulated.
32 devices in a mesh: segment: 2 (over x), dp: 4 (over z), mp: 4 (over y, core).
Axes of the slice: x: 2, y: 2, z: 4, core: 2. Of those that a mesh axis runs over, the one named last changes fastest.
Arguments:
- patch_tokens: bfloat16 [32, 16, 3072], P('dp', None, 'mp'), may hold values from -400 to 400
- visible_index: int32 [32, 16], P('dp'), may hold values from 0 to 63, as said below
- output_grad: bfloat16 [32, 16, 3072], P('dp', None, 'mp'), may hold values from -1.5 to 1.5
- norm_gain: float32 [2, 3072], P('segment'), may hold values from 0.1 to 1.9
- master_weights: float32 [2, 12288, 2048], P('segment', 'dp', 'mp'), may hold values from -2 to 2
- first_moment: float32 [2, 12288, 2048], P('segment', 'dp', 'mp'), may hold values from -6 to 6
- second_moment: float32 [2, 12288, 2048], P('segment', 'dp', 'mp'), may hold values from 0.01 to 1
Outputs:
- new_master: float32 [2, 12288, 2048], P('segment', 'dp', 'mp')
- new_first: float32 [2, 12288, 2048], P('segment', 'dp', 'mp')
- new_second: float32 [2, 12288, 2048], P('segment', 'dp', 'mp')
Inputs may be any that keep to these rules, and one draw needn't show every extreme that they name: `visible_index`: in each volume the 16 indices are distinct and increasing.
All inputs are finite; a program needn't handle non-finite values.
Results may differ from a plain program's by a relative error of at most 0.02.
Values may be sent and summed in bfloat16 or wider, within the bound.
A program may use at most 192 MiB of HBM per device.

v0:
```python
import math
import jax
import jax.numpy as jnp
from jax import lax
from jax.sharding import PartitionSpec as P

HD = 128
MB_VOLS = 2
beta_one = 0.9
beta_two = 0.95
learn_rate = 0.01
decay_rate = 0.1
adam_eps = 1e-08
norm_eps = 1e-05
step_count = 10


def from_behind(array, axis, by):
    peers = lax.axis_size(axis)
    pairs = [(i, i + by) for i in range(peers) if 0 <= i + by < peers]
    return lax.ppermute(array, axis, pairs)


def position_table(visible_index, model_width):
    half_width = model_width // 2
    angle_rate = jnp.exp(
        jnp.arange(half_width, dtype=jnp.float32) * (-2.0 * math.log(10000.0) / model_width)
    )
    angles = visible_index.astype(jnp.float32)[..., None] * angle_rate
    return jnp.concatenate([jnp.sin(angles), jnp.cos(angles)], axis=-1)


def norm_forward(hidden, norm_scale):
    values = hidden.astype(jnp.float32)
    centred = values - jnp.mean(values, axis=-1, keepdims=True)
    inverse_dev = lax.rsqrt(jnp.mean(centred * centred, axis=-1, keepdims=True) + norm_eps)
    standard = centred * inverse_dev
    return ((standard * norm_scale).astype(jnp.bfloat16), standard, inverse_dev)


def norm_backward(d_normed, d_output, standard, inverse_dev, norm_scale):
    scaled = d_normed * norm_scale
    inner = (
        scaled
        - jnp.mean(scaled, axis=-1, keepdims=True)
        - standard * jnp.mean(scaled * standard, axis=-1, keepdims=True)
    )
    return (d_output.astype(jnp.float32) + inner * inverse_dev).astype(jnp.bfloat16)


def softmax_rows(scores):
    lifted = jnp.exp(scores - jnp.max(scores, axis=-1, keepdims=True))
    return lifted / jnp.sum(lifted, axis=-1, keepdims=True)


def rounded(values):
    return lax.optimization_barrier(values.astype(jnp.bfloat16)).astype(jnp.float32)


def adam_update(gradient, master, first_moment, second_moment):
    new_first = beta_one * first_moment + (1.0 - beta_one) * gradient
    new_second = beta_two * second_moment + (1.0 - beta_two) * gradient * gradient
    direction = (
        new_first
        / (1.0 - beta_one**step_count)
        / (jnp.sqrt(new_second / (1.0 - beta_two**step_count)) + adam_eps)
    )
    new_master = master - learn_rate * (direction + decay_rate * master)
    return (new_master, new_first, new_second)


def layer_local(layer_in, norm_scale, weights):
    row_count, model_width = layer_in.shape
    col_count = weights.shape[1]
    head_count = col_count // HD
    length = row_count // MB_VOLS
    normed, standard, inverse_dev = norm_forward(layer_in, norm_scale)
    triple = weights[: 3 * model_width].reshape(3, model_width, col_count)
    project = jnp.einsum("nd,sdc->nsc", normed, triple, preferred_element_type=jnp.float32).astype(
        jnp.bfloat16
    )
    shaped = project.reshape(MB_VOLS, length, 3, head_count, HD)
    scores = jnp.einsum(
        "vqhe,vkhe->vhqk", shaped[:, :, 0], shaped[:, :, 1], preferred_element_type=jnp.float32
    ) * (1.0 / math.sqrt(HD))
    softmaxed = softmax_rows(scores)
    probs_half = softmaxed.astype(jnp.bfloat16)
    attended = jnp.einsum(
        "vhqk,vkhe->vqhe", probs_half, shaped[:, :, 2], preferred_element_type=jnp.float32
    )
    attended = attended.astype(jnp.bfloat16).reshape(row_count, col_count)
    return (normed, standard, inverse_dev, project, softmaxed, probs_half, attended)


def head_terms(attended, weights, model_width):
    return rounded(
        jnp.einsum(
            "nc,dc->nd", attended, weights[3 * model_width :], preferred_element_type=jnp.float32
        )
    )


def attention_back(d_output, saved_vals, weights):
    project, softmaxed, probs_half = (saved_vals[3], saved_vals[4], saved_vals[5])
    row_count, model_width = d_output.shape
    col_count = weights.shape[1]
    head_count = col_count // HD
    length = row_count // MB_VOLS
    shaped = project.reshape(MB_VOLS, length, 3, head_count, HD)
    d_attended = jnp.einsum(
        "nd,dc->nc", d_output, weights[3 * model_width :], preferred_element_type=jnp.float32
    )
    d_attended = d_attended.astype(jnp.bfloat16).reshape(MB_VOLS, length, head_count, HD)
    d_probs = jnp.einsum(
        "vqhe,vkhe->vhqk", d_attended, shaped[:, :, 2], preferred_element_type=jnp.float32
    )
    d_scores = (
        softmaxed
        * (d_probs - jnp.sum(d_probs * softmaxed, axis=-1, keepdims=True))
        * (1.0 / math.sqrt(HD))
    ).astype(jnp.bfloat16)
    d_queries = jnp.einsum(
        "vhqk,vkhe->vqhe", d_scores, shaped[:, :, 1], preferred_element_type=jnp.float32
    ).astype(jnp.bfloat16)
    d_keys = jnp.einsum(
        "vhqk,vqhe->vkhe", d_scores, shaped[:, :, 0], preferred_element_type=jnp.float32
    ).astype(jnp.bfloat16)
    d_values = jnp.einsum(
        "vhqk,vqhe->vkhe", probs_half, d_attended, preferred_element_type=jnp.float32
    ).astype(jnp.bfloat16)
    return jnp.stack([d_queries, d_keys, d_values], axis=2).reshape(row_count, 3, col_count)


def feature_terms(d_project, weights, model_width):
    col_count = weights.shape[1]
    triple = weights[: 3 * model_width].reshape(3, model_width, col_count)
    return rounded(jnp.einsum("nsc,sdc->nd", d_project, triple, preferred_element_type=jnp.float32))


def shards(
    patch_tokens, visible_index, output_grad, norm_gain, master_weights, first_moment, second_moment
):
    model_width = patch_tokens.shape[2] * lax.axis_size("mp")
    rows_here = master_weights.shape[1]
    is_first = lax.axis_index("segment") == 0
    norm_scale = norm_gain[0]
    weights = lax.all_gather(master_weights[0].astype(jnp.bfloat16), "dp", axis=0, tiled=True)
    tokens_full, grads_full = (
        lax.all_gather(patch_tokens, "mp", axis=2, tiled=True),
        lax.all_gather(output_grad, "mp", axis=2, tiled=True),
    )
    vol_count, length = visible_index.shape
    micro_count = vol_count // MB_VOLS
    mb_rows = MB_VOLS * length
    first_inputs = (
        tokens_full.astype(jnp.float32) + position_table(visible_index, model_width)
    ).astype(jnp.bfloat16)
    first_inputs = first_inputs.reshape(micro_count, mb_rows, model_width)
    out_grads = grads_full.reshape(micro_count, mb_rows, model_width)
    zeros_full = jnp.zeros((mb_rows, model_width), jnp.bfloat16)
    saved_ticks = []
    received = zeros_full
    for step_index in range(micro_count + 1):
        arriving = received
        own_input = first_inputs[step_index] if step_index < micro_count else zeros_full
        layer_in = jnp.where(is_first, own_input, arriving)
        saved_vals = layer_local(layer_in, norm_scale, weights)
        saved_ticks.append(saved_vals)
        if step_index < micro_count:
            head_part = head_terms(saved_vals[6], weights, model_width)
            mixed = lax.psum(head_part.astype(jnp.bfloat16), "mp").astype(jnp.float32)
            layer_out = (layer_in.astype(jnp.float32) + mixed).astype(jnp.bfloat16)
            received = from_behind(layer_out, "segment", 1)
    back_ticks = []
    for step_index in range(micro_count + 1):
        arriving = received if step_index > 0 else zeros_full
        own_grad = (
            out_grads[micro_count - 1 - step_index] if step_index < micro_count else zeros_full
        )
        d_output = jnp.where(is_first, arriving, own_grad)
        saved_vals = saved_ticks[micro_count - step_index]
        d_project = attention_back(d_output, saved_vals, weights)
        back_ticks.append((d_output, d_project))
        if step_index < micro_count:
            d_terms = feature_terms(d_project, weights, model_width)
            standard, inverse_dev = (saved_vals[1], saved_vals[2])
            summed = lax.psum(d_terms.astype(jnp.bfloat16), "mp").astype(jnp.float32)
            d_input = norm_backward(summed, d_output, standard, inverse_dev, norm_scale)
            received = from_behind(d_input, "segment", -1)
    all_steps = range(micro_count + 1)
    normed_ticks = jnp.stack([saved_ticks[micro_count - step_index][0] for step_index in all_steps])
    attended_ticks = jnp.stack(
        [saved_ticks[micro_count - step_index][6] for step_index in all_steps]
    )
    d_output_ticks = jnp.stack([back_ticks[step_index][0] for step_index in all_steps])
    d_project_ticks = jnp.stack([back_ticks[step_index][1] for step_index in all_steps])
    right_ticks = jnp.concatenate([d_project_ticks, attended_ticks[:, :, None]], axis=2)

    def pick_valid(ticks):
        chosen = jnp.where(is_first, ticks[1:], ticks[:-1])
        return chosen.reshape((micro_count * mb_rows,) + ticks.shape[2:])

    normed_all = pick_valid(normed_ticks)
    d_output_all = pick_valid(d_output_ticks)
    right_all = pick_valid(right_ticks)

    def one_piece(piece_index):
        first_row = piece_index * rows_here
        part_index = first_row // model_width
        col_offset = first_row % model_width
        left_norm = lax.dynamic_slice_in_dim(normed_all, col_offset, rows_here, 1)
        left_grad = lax.dynamic_slice_in_dim(d_output_all, col_offset, rows_here, 1)
        left_side = jnp.where(part_index == 3, left_grad, left_norm)
        right_side = lax.dynamic_index_in_dim(right_all, part_index, 1, keepdims=False)
        return jnp.einsum("tr,tc->rc", left_side, right_side, preferred_element_type=jnp.float32)

    blocks = lax.map(
        one_piece, jnp.arange(rows_here * lax.axis_size("dp") // rows_here, dtype=jnp.int32)
    )
    gradient = lax.psum_scatter(
        blocks.reshape(rows_here * lax.axis_size("dp"), blocks.shape[2]).astype(jnp.bfloat16),
        "dp",
        scatter_dimension=0,
        tiled=True,
    ).astype(jnp.float32)
    new_master, new_first, new_second = adam_update(
        gradient, master_weights[0], first_moment[0], second_moment[0]
    )
    return (new_master[None], new_first[None], new_second[None])


def solution(mesh):
    placed = (
        P("dp", None, "mp"),
        P("dp", None),
        P("dp", None, "mp"),
        P("segment", None),
        P("segment", "dp", "mp"),
        P("segment", "dp", "mp"),
        P("segment", "dp", "mp"),
    )
    return jax.shard_map(
        shards,
        mesh=mesh,
        in_specs=placed,
        out_specs=(P("segment", "dp", "mp"), P("segment", "dp", "mp"), P("segment", "dp", "mp")),
        check_vma=False,
    )
```

profile of v0, /device:TPU:0, one launch (start us, length us, event | category | flops | bytes accessed | tf_op | source)
XLA Modules:
  0.0 909.8 jit_solution(2568975783798834956)
XLA Ops:
  7.2 4.9 bitcast_convert_fusion
  12.3 10.1 %all_gather.10 = bf16[8,16,3072]{2,1,0:T(8,128)(2,1)S(1)} all-gather(bf16[8,16,768]{2,1,0:T(8,128)(2,1)S(1)} %copy-done.3), channel_id=1, replica_groups=mesh['segment'=2,'dp'=4,'mp'=4] {'mp'}, dimensions={2}, use_global_device_ids=true | all-gather | bytes 983040 | tf_op jit(solution)/shard_map/all_gather | solution.py:149
  22.3 2.8 multiply_sine_fusion
  25.8 207.5 %all-gather.2.cloned.1.call-done = bf16[12288,512]{1,0:T(8,128)(2,1)} async-done(((bf16[3072,512]{1,0:T(8,128)(2,1)}), bf16[12288,512]{1,0:T(8,128)(2,1)}) %all-gather.2.cloned.1.call-update) | async-done | bytes 12582928 | tf_op jit(solution)/shard_map/all_gather | solution.py:147
  233.2 5.2 slice.160
  238.5 3.6 copy-done
  244.9 3.6 convolution_convert_fusion.3
  248.6 30.0 %all-reduce.9.cloned.1.call-done = bf16[32,3072]{1,0:T(8,128)(2,1)} async-done(((bf16[32,3072]{1,0:T(8,128)(2,1)}), bf16[32,3072]{1,0:T(8,128)(2,1)}) %all-reduce.9.cloned.1.call-update) | async-done | bytes 196624 | tf_op jit(solution)/shard_map/psum | solution.py:171
  279.6 3.4 collective-permute-start
  283.0 3.1 collective-permute-done
  286.6 5.5 convolution_convert_fusion.7
  293.3 3.6 convolution_convert_fusion.2
  297.0 33.0 %all-reduce.11.cloned.1.call-done = bf16[32,3072]{1,0:T(8,128)(2,1)} async-done(((bf16[32,3072]{1,0:T(8,128)(2,1)}), bf16[32,3072]{1,0:T(8,128)(2,1)}) %all-reduce.11.cloned.1.call-update) | async-done | bytes 196624 | tf_op jit(solution)/shard_map/psum | solution.py:171
  330.9 3.4 collective-permute-start.1
  334.3 3.2 collective-permute-done.1
  337.9 5.5 convolution_convert_fusion.6
  344.7 3.6 convolution_convert_fusion.1
  348.4 7.8 all_gather.9
  356.2 25.1 %all-reduce.13.cloned.1.call-done = bf16[32,3072]{1,0:T(8,128)(2,1)} async-done(((bf16[32,3072]{1,0:T(8,128)(2,1)}), bf16[32,3072]{1,0:T(8,128)(2,1)}) %all-reduce.13.cloned.1.call-update) | async-done | bytes 196624 | tf_op jit(solution)/shard_map/psum | solution.py:171
  382.3 3.6 collective-permute-start.2
  386.1 2.8 collective-permute-done.2
  389.3 5.5 convolution_convert_fusion.5
  395.4 3.6 convolution_convert_fusion
  399.8 32.2 %all-reduce.15.cloned.1.call-done = bf16[32,3072]{1,0:T(8,128)(2,1)} async-done(((bf16[32,3072]{1,0:T(8,128)(2,1)}), bf16[32,3072]{1,0:T(8,128)(2,1)}) %all-reduce.15.cloned.1.call-update) | async-done | bytes 196624 | tf_op jit(solution)/shard_map/psum | solution.py:171
  433.0 3.4 collective-permute-start.3
  440.0 5.5 convolution_convert_fusion.4
  446.7 7.2 fusion.21
  456.2 30.7 %all-reduce.17.cloned.1.call-done = bf16[32,3072]{1,0:T(8,128)(2,1)} async-done(((bf16[32,3072]{1,0:T(8,128)(2,1)}), bf16[32,3072]{1,0:T(8,128)(2,1)}) %all-reduce.17.cloned.1.call-update) | async-done | bytes 196624 | tf_op jit(solution)/shard_map/psum | solution.py:187
  490.5 6.2 collective-permute-done.4
  496.8 2.5 convolution_convert_fusion.12
  500.4 7.2 fusion.22
  507.7 31.0 %all-reduce.19.cloned.1.call-done = bf16[32,3072]{1,0:T(8,128)(2,1)} async-done(((bf16[32,3072]{1,0:T(8,128)(2,1)}), bf16[32,3072]{1,0:T(8,128)(2,1)}) %all-reduce.19.cloned.1.call-update) | async-done | bytes 196624 | tf_op jit(solution)/shard_map/psum | solution.py:187
  542.4 6.2 collective-permute-done.5
  548.7 2.5 convolution_convert_fusion.11
  552.2 7.2 fusion.23
  559.6 30.9 %all-reduce.21.cloned.1.call-done = bf16[32,3072]{1,0:T(8,128)(2,1)} async-done(((bf16[32,3072]{1,0:T(8,128)(2,1)}), bf16[32,3072]{1,0:T(8,128)(2,1)}) %all-reduce.21.cloned.1.call-update) | async-done | bytes 196624 | tf_op jit(solution)/shard_map/psum | solution.py:187
  594.5 5.9 collective-permute-done.6
  600.5 2.5 convolution_convert_fusion.10
  604.1 7.2 fusion.24
  611.4 31.0 %all-reduce.23.cloned.1.call-done = bf16[32,3072]{1,0:T(8,128)(2,1)} async-done(((bf16[32,3072]{1,0:T(8,128)(2,1)}), bf16[32,3072]{1,0:T(8,128)(2,1)}) %all-reduce.23.cloned.1.call-update) | async-done | bytes 196624 | tf_op jit(solution)/shard_map/psum | solution.py:187
  646.3 6.1 collective-permute-done.7
  659.7 15.8 %while.12 = (s32[]{:T(128)}, bf16[4,3072,512]{2,1,0:T(8,128)(2,1)}, s32[4]{0:T(128)S(1)}, bf16[128,3072]{1,0:T(8,128)(2,1)S(1)}, bf16[128,3072]{1,0:T(8,128)(2,1...) while((s32[]{:T(128)}, bf16[4,3072,512]{2,1,0:T(8,128)(2,1)}, ...), condition=%wide.region_42.43_spmd, body=%wide.region_41.42_spmd.sunk | while | flops 403046400 | bytes 7996187 | solution.py:217
  661.0 2.7 bitcast_dynamic-update-slice_fusion.2
  664.9 2.7 bitcast_dynamic-update-slice_fusion.2
  668.8 2.7 bitcast_dynamic-update-slice_fusion.2
  672.8 2.7 bitcast_dynamic-update-slice_fusion.2
  675.5 211.3 %reduce-scatter.2.cloned.1.call-done = bf16[3072,512]{1,0:T(8,128)(2,1)} async-done(((bf16[12288,512]{1,0:T(8,128)(2,1)}), bf16[3072,512]{1,0:T(8,128)(2,1)}) %reduce-scatter.2.cloned.1.call-update) | async-done | bytes 3145744 | tf_op jit(solution)/shard_map/reduce_scatter | solution.py:220
  886.8 16.1 %fusion.25 = (f32[1,3072,512]{2,1,0:T(8,128)}, f32[1,3072,512]{2,1,0:T(8,128)}, f32[1,3072,512]{2,1,0:T(8,128)}) fusion(bf16[3072,512]{1,0:T(8,128)(2,1)} %reduce-scatter.2.cloned.1.call-done, f32[1,3072,512]{2,1,0:T(8,128)} %param.15, f32[1,3072,512]{2,1,0:T(8,128)} %param.14, f32[1,3072,512]{2,1,0:T(8,128)} %param.13), kind=kLoop, calls=%fused_computation.39 | loop fusion | flops 25165824 | bytes 40894464 | tf_op jit(solution)/shard_map/broadcast_in_dim | solution.py:229
  (268 shorter events, 47.9 us)
Async XLA Ops:
  7.2 5.1 copy-start.3
  7.2 226.1 %all-gather.2.cloned.1.call-start = ((), (), s32[]{:S(2)}) async-start(), calls=%async_computation.1 | async-start | bytes 15728640 | tf_op jit(solution)/shard_map/all_gather | solution.py:147
  12.1 13.5 %copy-start.1 = (f32[1,3072]{1,0:T(1,128)S(1)}, f32[1,3072]{1,0:T(1,128)}, u32[]{:S(2)}) copy-start(f32[1,3072]{1,0:T(1,128)} %param.12) | copy-start | bytes 36868
  12.2 266.4 %all-reduce.9.cloned.1.call-start = ((), (), s32[]{:S(2)}) async-start(), calls=%async_computation.2 | async-start | bytes 393216 | tf_op jit(solution)/shard_map/psum | solution.py:171
  243.7 34.8 %copy-start.17 = (bf16[2,16,1,4,128]{4,3,1,0,2:T(4,128)(2,1)}, bf16[2,16,1,4,128]{4,3,1,0,2:T(4,128)(2,1)S(1)}, u32[]{:S(2)}) copy-start(bf16[2,16,1,4,128]{4,3,1,0,2:T(4,128)(2,1)S(1)} %get-tuple-element.136) | copy-start | bytes 98308
  243.7 35.8 %copy-start.9 = (bf16[2,16,1,4,128]{4,3,1,0,2:T(4,128)(2,1)}, bf16[2,16,1,4,128]{4,3,1,0,2:T(4,128)(2,1)S(1)}, u32[]{:S(2)}) copy-start(bf16[2,16,1,4,128]{4,3,1,0,2:T(4,128)(2,1)S(1)} %get-tuple-element.137) | copy-start | bytes 98308
  243.8 35.8 %copy-start.15 = (bf16[2,16,1,4,128]{4,3,1,0,2:T(4,128)(2,1)}, bf16[2,16,1,4,128]{4,3,1,0,2:T(4,128)(2,1)S(1)}, u32[]{:S(2)}) copy-start(bf16[2,16,1,4,128]{4,3,1,0,2:T(4,128)(2,1)S(1)} %get-tuple-element.135) | copy-start | bytes 98308
  244.6 35.0 %copy-start.30 = (f32[2,4,16]{2,1,0:T(4,128)}, f32[2,4,16]{2,1,0:T(4,128)S(1)}, u32[]{:S(2)}) copy-start(f32[2,4,16]{2,1,0:T(4,128)S(1)} %get-tuple-element.140) | copy-start | bytes 1540
  248.5 81.4 %all-reduce.11.cloned.1.call-start = ((), (), s32[]{:S(2)}) async-start(), calls=%async_computation.3 | async-start | bytes 393216 | tf_op jit(solution)/shard_map/psum | solution.py:171
  279.6 6.6 collective-permute-start
  292.1 37.8 %copy-start.21 = (bf16[2,16,1,4,128]{4,3,1,0,2:T(4,128)(2,1)}, bf16[2,16,1,4,128]{4,3,1,0,2:T(4,128)(2,1)S(1)}, u32[]{:S(2)}) copy-start(bf16[2,16,1,4,128]{4,3,1,0,2:T(4,128)(2,1)S(1)} %get-tuple-element.133) | copy-start | bytes 98308
  292.9 44.7 %copy-start.32 = (f32[2,4,16]{2,1,0:T(4,128)}, f32[2,4,16]{2,1,0:T(4,128)S(1)}, u32[]{:S(2)}) copy-start(f32[2,4,16]{2,1,0:T(4,128)S(1)} %get-tuple-element.142) | copy-start | bytes 1540
  296.9 84.4 %all-reduce.13.cloned.1.call-start = ((), (), s32[]{:S(2)}) async-start(), calls=%async_computation.4 | async-start | bytes 393216 | tf_op jit(solution)/shard_map/psum | solution.py:171
  330.9 6.6 collective-permute-start.1
  337.9 10.4 %copy-start.4 = (bf16[8,16,768]{2,1,0:T(8,128)(2,1)S(1)}, bf16[8,16,768]{2,1,0:T(8,128)(2,1)}, u32[]{:S(2)}) copy-start(bf16[8,16,768]{2,1,0:T(8,128)(2,1)} %param.11) | copy-start | bytes 589828
  343.5 38.8 %copy-start.23 = (bf16[2,16,1,4,128]{4,3,1,0,2:T(4,128)(2,1)}, bf16[2,16,1,4,128]{4,3,1,0,2:T(4,128)(2,1)S(1)}, u32[]{:S(2)}) copy-start(bf16[2,16,1,4,128]{4,3,1,0,2:T(4,128)(2,1)S(1)} %get-tuple-element.129) | copy-start | bytes 98308
  343.5 38.8 %copy-start.25 = (bf16[2,16,1,4,128]{4,3,1,0,2:T(4,128)(2,1)}, bf16[2,16,1,4,128]{4,3,1,0,2:T(4,128)(2,1)S(1)}, u32[]{:S(2)}) copy-start(bf16[2,16,1,4,128]{4,3,1,0,2:T(4,128)(2,1)S(1)} %get-tuple-element.130) | copy-start | bytes 98308
  344.3 38.0 %copy-start.34 = (f32[2,4,16]{2,1,0:T(4,128)}, f32[2,4,16]{2,1,0:T(4,128)S(1)}, u32[]{:S(2)}) copy-start(f32[2,4,16]{2,1,0:T(4,128)S(1)} %get-tuple-element.144) | copy-start | bytes 1540
  348.3 83.8 %all-reduce.15.cloned.1.call-start = ((), (), s32[]{:S(2)}) async-start(), calls=%async_computation.5 | async-start | bytes 393216 | tf_op jit(solution)/shard_map/psum | solution.py:171
  382.3 6.6 collective-permute-start.2
  399.0 87.9 %all-reduce.17.cloned.1.call-start = ((), (), s32[]{:S(2)}) async-start(), calls=%async_computation.6 | async-start | bytes 393216 | tf_op jit(solution)/shard_map/psum | solution.py:187
  433.0 6.6 collective-permute-start.3
  453.9 84.9 %all-reduce.19.cloned.1.call-start = ((), (), s32[]{:S(2)}) async-start(), calls=%async_computation.7 | async-start | bytes 393216 | tf_op jit(solution)/shard_map/psum | solution.py:187
  489.2 7.6 collective-permute-start.4
  500.3 42.1 %copy-start.6 = (bf16[1,32,1,512]{3,1,2,0:T(8,128)(2,1)S(1)}, bf16[1,32,1,512]{3,1,2,0:T(8,128)(2,1)}, u32[]{:S(2)}) copy-start(bf16[1,32,1,512]{3,1,2,0:T(8,128)(2,1)} %stack.162) | copy-start | bytes 98308
  500.3 42.1 %copy-start.7 = (bf16[1,32,1,512]{3,1,2,0:T(8,128)(2,1)S(1)}, bf16[1,32,1,512]{3,1,2,0:T(8,128)(2,1)}, u32[]{:S(2)}) copy-start(bf16[1,32,1,512]{3,1,2,0:T(8,128)(2,1)} %stack.163) | copy-start | bytes 98308
  500.3 42.1 %copy-start.8 = (bf16[1,32,1,512]{3,1,2,0:T(8,128)(2,1)S(1)}, bf16[1,32,1,512]{3,1,2,0:T(8,128)(2,1)}, u32[]{:S(2)}) copy-start(bf16[1,32,1,512]{3,1,2,0:T(8,128)(2,1)} %stack.164) | copy-start | bytes 98308
  500.4 50.9 %copy-start.14 = (bf16[2,16,1,4,128]{4,3,1,0,2:T(4,128)(2,1)S(1)}, bf16[2,16,1,4,128]{4,3,1,0,2:T(4,128)(2,1)}, u32[]{:S(2)}) copy-start(bf16[2,16,1,4,128]{4,3,1,0,2:T(4,128)(2,1)} %copy-done.13) | copy-start | bytes 98308
  500.4 51.0 %copy-start.24 = (bf16[2,16,1,4,128]{4,3,1,0,2:T(4,128)(2,1)S(1)}, bf16[2,16,1,4,128]{4,3,1,0,2:T(4,128)(2,1)}, u32[]{:S(2)}) copy-start(bf16[2,16,1,4,128]{4,3,1,0,2:T(4,128)(2,1)} %copy-done.23) | copy-start | bytes 98308
  500.4 51.0 %copy-start.29 = (f32[2,4,16,16]{2,3,1,0:T(8,128)S(1)}, f32[2,4,16,16]{2,3,1,0:T(8,128)}, u32[]{:S(2)}) copy-start(f32[2,4,16,16]{2,3,1,0:T(8,128)} %get-tuple-element.145) | copy-start | bytes 24580
  500.4 51.0 %copy-start.35 = (f32[2,4,16]{2,1,0:T(4,128)S(1)}, f32[2,4,16]{2,1,0:T(4,128)}, u32[]{:S(2)}) copy-start(f32[2,4,16]{2,1,0:T(4,128)} %copy-done.34) | copy-start | bytes 1540
  507.6 44.0 %copy-start.26 = (bf16[2,16,1,4,128]{4,3,1,0,2:T(4,128)(2,1)S(1)}, bf16[2,16,1,4,128]{4,3,1,0,2:T(4,128)(2,1)}, u32[]{:S(2)}) copy-start(bf16[2,16,1,4,128]{4,3,1,0,2:T(4,128)(2,1)} %copy-done.25) | copy-start | bytes 98308
  507.7 82.9 %all-reduce.21.cloned.1.call-start = ((), (), s32[]{:S(2)}) async-start(), calls=%async_computation.8 | async-start | bytes 393216 | tf_op jit(solution)/shard_map/psum | solution.py:187
  541.1 7.6 collective-permute-start.5
  552.2 7.3 copy-start.5
  559.4 43.6 %copy-start.12 = (bf16[2,16,1,4,128]{4,3,1,0,2:T(4,128)(2,1)S(1)}, bf16[2,16,1,4,128]{4,3,1,0,2:T(4,128)(2,1)}, u32[]{:S(2)}) copy-start(bf16[2,16,1,4,128]{4,3,1,0,2:T(4,128)(2,1)} %copy-done.11) | copy-start | bytes 98308
  559.4 43.8 %copy-start.20 = (bf16[2,16,1,4,128]{4,3,1,0,2:T(4,128)(2,1)S(1)}, bf16[2,16,1,4,128]{4,3,1,0,2:T(4,128)(2,1)}, u32[]{:S(2)}) copy-start(bf16[2,16,1,4,128]{4,3,1,0,2:T(4,128)(2,1)} %copy-done.19) | copy-start | bytes 98308
  559.4 43.8 %copy-start.28 = (f32[2,4,16,16]{2,3,1,0:T(8,128)S(1)}, f32[2,4,16,16]{2,3,1,0:T(8,128)}, u32[]{:S(2)}) copy-start(f32[2,4,16,16]{2,3,1,0:T(8,128)} %get-tuple-element.143) | copy-start | bytes 24580
  559.4 43.8 %copy-start.33 = (f32[2,4,16]{2,1,0:T(4,128)S(1)}, f32[2,4,16]{2,1,0:T(4,128)}, u32[]{:S(2)}) copy-start(f32[2,4,16]{2,1,0:T(4,128)} %copy-done.32) | copy-start | bytes 1540
  559.4 44.0 %copy-start.22 = (bf16[2,16,1,4,128]{4,3,1,0,2:T(4,128)(2,1)S(1)}, bf16[2,16,1,4,128]{4,3,1,0,2:T(4,128)(2,1)}, u32[]{:S(2)}) copy-start(bf16[2,16,1,4,128]{4,3,1,0,2:T(4,128)(2,1)} %copy-done.21) | copy-start | bytes 98308
  559.5 83.0 %all-reduce.23.cloned.1.call-start = ((), (), s32[]{:S(2)}) async-start(), calls=%async_computation.9 | async-start | bytes 393216 | tf_op jit(solution)/shard_map/psum | solution.py:187
  592.9 7.6 collective-permute-start.6
  611.3 44.3 %copy-start.10 = (bf16[2,16,1,4,128]{4,3,1,0,2:T(4,128)(2,1)S(1)}, bf16[2,16,1,4,128]{4,3,1,0,2:T(4,128)(2,1)}, u32[]{:S(2)}) copy-start(bf16[2,16,1,4,128]{4,3,1,0,2:T(4,128)(2,1)} %copy-done.9) | copy-start | bytes 98308
  611.3 44.4 %copy-start.16 = (bf16[2,16,1,4,128]{4,3,1,0,2:T(4,128)(2,1)S(1)}, bf16[2,16,1,4,128]{4,3,1,0,2:T(4,128)(2,1)}, u32[]{:S(2)}) copy-start(bf16[2,16,1,4,128]{4,3,1,0,2:T(4,128)(2,1)} %copy-done.15) | copy-start | bytes 98308
  611.3 44.4 %copy-start.31 = (f32[2,4,16]{2,1,0:T(4,128)S(1)}, f32[2,4,16]{2,1,0:T(4,128)}, u32[]{:S(2)}) copy-start(f32[2,4,16]{2,1,0:T(4,128)} %copy-done.30) | copy-start | bytes 1540
  611.3 45.6 %copy-start.18 = (bf16[2,16,1,4,128]{4,3,1,0,2:T(4,128)(2,1)S(1)}, bf16[2,16,1,4,128]{4,3,1,0,2:T(4,128)(2,1)}, u32[]{:S(2)}) copy-start(bf16[2,16,1,4,128]{4,3,1,0,2:T(4,128)(2,1)} %copy-done.17) | copy-start | bytes 98308
  611.3 275.4 %reduce-scatter.2.cloned.1.call-start = ((), (), s32[]{:S(2)}) async-start(), calls=%async_computation.10 | async-start | bytes 15728640 | tf_op jit(solution)/shard_map/reduce_scatter | solution.py:220
  644.8 7.6 collective-permute-start.7
  (6 other events, 19.8 us)
Sparse Core Ops, SparseCore 0:
  12.3 220.9 all-gather.1
  248.7 29.8 all-reduce.8
  297.0 32.8 all-reduce.10
  348.4 32.8 all-reduce.12
  399.1 32.8 all-reduce.14
  454.0 32.8 all-reduce.16
  507.8 30.9 all-reduce.18
  559.6 30.9 all-reduce.20
  611.5 30.9 all-reduce.22
  675.6 211.1 reduce-scatter.1
where the time goes:
time: 911 us; the launch traced here: 910 us
  waiting for transfers between devices  697 us (77%)
  matrix products  100 us (11%)
  other arithmetic  41.1 us (5%)
  starting transfers between devices  19.5 us (2%)
  blocking collectives  17.9 us (2%)
  local copies, waits for them, and re-layouts  16 us (2%)
  between operations  15.4 us (2%)
    reduce_scatter x1, waiting for transfers between devices, shards(): lax.psum_scatter(blocks.reshape(rows_here * lax.axis_size('dp'), blocks.s...  211 us
    all_gather x1, waiting for transfers between devices, shards(): lax.all_gather(master_weights[0].astype(jnp.bfloat16), 'dp', axis=0, tile...  207 us
    psum x4, waiting for transfers between devices, shards(): summed = lax.psum(d_terms.astype(jnp.bfloat16), 'mp').astype(jnp.float32)  124 us
    psum x4, waiting for transfers between devices, shards(): mixed = lax.psum(head_part.astype(jnp.bfloat16), 'mp').astype(jnp.float32)  120 us
    ppermute x8, waiting for transfers between devices, from_behind(): return lax.ppermute(array, axis, pairs)  34 us
    dot_general x4, matrix products, feature_terms(): jnp.einsum('nsc,sdc->nd', d_project, triple, preferred_element_type=jnp.f...  28.8 us
    dot_general x5, matrix products, layer_local(): jnp.einsum('nd,sdc->nsc', normed, triple, preferred_element_type=jnp.floa...  23.5 us
    ppermute x8, starting transfers between devices, from_behind(): return lax.ppermute(array, axis, pairs)  19.1 us
  transfers between devices with their start and end apart: 18, of which 18 were waited for; matrix products, arithmetic and copies ran while one was open for 1% of the time, Pallas kernels for 0%

commit v1 on v0

--- a/solution.py
+++ b/solution.py
@@ -168,7 +168,12 @@
         saved_ticks.append(saved_vals)
         if step_index < micro_count:
             head_part = head_terms(saved_vals[6], weights, model_width)
-            mixed = lax.psum(head_part.astype(jnp.bfloat16), "mp").astype(jnp.float32)
+
+            def draft_the_chains(vector, along_axis="mp"):
+                later = jnp.sum(lax.all_gather(vector, axis_name=along_axis), 0)
+                return later
+
+            mixed = draft_the_chains(head_part.astype(jnp.bfloat16)).astype(jnp.float32)
             layer_out = (layer_in.astype(jnp.float32) + mixed).astype(jnp.bfloat16)
             received = from_behind(layer_out, "segment", 1)
     back_ticks = []

time: 911 us -> 818 us (0.90)
  waiting for transfers between devices: 697 us -> 574 us
  blocking collectives: 17.9 us -> 52.3 us
    psum x4 -> x0, waiting for transfers between devices: 120 us -> none  [shards(): mixed = lax.psum(head_part.astype(jnp.bfloat16), 'mp').astype(jnp.float32)]
    all_gather x0 -> x4, blocking collectives: none -> 33.8 us  [draft_the_chains(): later = jnp.sum(lax.all_gather(vector, axis_name=along_axis), 0)]
  transfers between devices with their start and end apart: 18 -> 14, of which waited for: 18 -> 13; matrix products, arithmetic and copies ran while one was open for 1% -> 1% of each run, Pallas kernels for 0% -> 0%
where the time goes in v1:
time: 818 us; the launch traced here: 817 us
  waiting for transfers between devices  574 us (70%)
  matrix products  96.2 us (12%)
  blocking collectives  52.3 us (6%)
  other arithmetic  41.5 us (5%)
  starting transfers between devices  19.4 us (2%)
  between operations  15.4 us (2%)
  local copies, waits for them, and re-layouts  14.9 us (2%)
    reduce_scatter x1, waiting for transfers between devices, shards(): lax.psum_scatter(blocks.reshape(rows_here * lax.axis_size('dp'), blocks.s...  211 us
    all_gather x1, waiting for transfers between devices, shards(): lax.all_gather(master_weights[0].astype(jnp.bfloat16), 'dp', axis=0, tile...  207 us
    psum x4, waiting for transfers between devices, shards(): summed = lax.psum(d_terms.astype(jnp.bfloat16), 'mp').astype(jnp.float32)  123 us
    all_gather x4, blocking collectives, draft_the_chains(): later = jnp.sum(lax.all_gather(vector, axis_name=along_axis), 0)  33.8 us
    ppermute x8, waiting for transfers between devices, from_behind(): return lax.ppermute(array, axis, pairs)  32.9 us
    dot_general x4, matrix products, feature_terms(): jnp.einsum('nsc,sdc->nd', d_project, triple, preferred_element_type=jnp.f...  28.9 us
    dot_general x5, matrix products, layer_local(): jnp.einsum('nd,sdc->nsc', normed, triple, preferred_element_type=jnp.floa...  23.4 us
    ppermute x8, starting transfers between devices, from_behind(): return lax.ppermute(array, axis, pairs)  19.1 us
  transfers between devices with their start and end apart: 14, of which 13 were waited for; matrix products, arithmetic and copies ran while one was open for 1% of the time, Pallas kernels for 0%

profile of v1, /device:TPU:0, one launch (start us, length us, event | category | flops | bytes accessed | tf_op | source)
XLA Modules:
  0.0 816.7 jit_solution(10002770978799164355)
XLA Ops:
  7.2 4.9 bitcast_convert_fusion
  12.3 10.1 %all_gather.34 = bf16[8,16,3072]{2,1,0:T(8,128)(2,1)S(1)} all-gather(bf16[8,16,768]{2,1,0:T(8,128)(2,1)S(1)} %copy-done.6), channel_id=1, replica_groups=mesh['segment'=2,'dp'=4,'mp'=4] {'mp'}, dimensions={2}, use_global_device_ids=true | all-gather | bytes 983040 | tf_op jit(solution)/shard_map/all_gather | solution.py:149
  22.3 2.8 multiply_sine_fusion
  26.5 206.7 %all-gather.6.cloned.1.call-done = bf16[12288,512]{1,0:T(8,128)(2,1)} async-done(((bf16[3072,512]{1,0:T(8,128)(2,1)}), bf16[12288,512]{1,0:T(8,128)(2,1)}) %all-gather.6.cloned.1.call-update) | async-done | bytes 12582928 | tf_op jit(solution)/shard_map/all_gather | solution.py:147
  233.2 5.2 slice.160
  238.5 3.6 copy-done
  244.9 2.9 convolution_convert_fusion.3
  247.8 8.5 %all-gather = bf16[128,3072]{1,0:T(8,128)(2,1)S(1)} all-gather(bf16[32,3072]{1,0:T(8,128)(2,1)S(1)} %convolution_convert_fusion.3), channel_id=2, replica_groups=mesh['segment'=2,'dp'=4,'mp'=4] {'mp'}, dimensions={0}, use_global_device_ids=true | all-gather | bytes 983040 | tf_op jit(solution)/shard_map/all_gather | solution.py:173
  256.6 3.4 collective-permute-start
  260.0 8.4 %all_gather.33 = bf16[8,16,3072]{2,1,0:T(8,128)(2,1)S(1)} all-gather(bf16[8,16,768]{2,1,0:T(8,128)(2,1)S(1)} %copy-done.7), channel_id=1, replica_groups=mesh['segment'=2,'dp'=4,'mp'=4] {'mp'}, dimensions={2}, use_global_device_ids=true | all-gather | bytes 983040 | tf_op jit(solution)/shard_map/all_gather | solution.py:150
  268.9 5.5 convolution_convert_fusion.7
  275.7 2.9 convolution_convert_fusion.2
  278.6 8.7 %all-gather.1 = bf16[128,3072]{1,0:T(8,128)(2,1)S(1)} all-gather(bf16[32,3072]{1,0:T(8,128)(2,1)S(1)} %convolution_convert_fusion.2), channel_id=3, replica_groups=mesh['segment'=2,'dp'=4,'mp'=4] {'mp'}, dimensions={0}, use_global_device_ids=true | all-gather | bytes 983040 | tf_op jit(solution)/shard_map/all_gather | solution.py:173
  289.3 4.4 collective-permute-done.1
  295.1 5.5 convolution_convert_fusion.6
  301.9 2.9 convolution_convert_fusion.1
  304.8 8.6 %all-gather.2 = bf16[128,3072]{1,0:T(8,128)(2,1)S(1)} all-gather(bf16[32,3072]{1,0:T(8,128)(2,1)S(1)} %convolution_convert_fusion.1), channel_id=4, replica_groups=mesh['segment'=2,'dp'=4,'mp'=4] {'mp'}, dimensions={0}, use_global_device_ids=true | all-gather | bytes 983040 | tf_op jit(solution)/shard_map/all_gather | solution.py:173
  313.6 4.4 collective-permute-start.2
  318.8 3.9 collective-permute-done.2
  323.1 5.5 convolution_convert_fusion.5
  330.4 2.9 convolution_convert_fusion
  333.3 7.9 all-gather.3
  341.5 4.4 collective-permute-start.3
  345.9 2.5 convolution_convert_fusion.13
  350.9 5.5 convolution_convert_fusion.4
  357.6 7.2 fusion.21
  365.4 30.2 %all-reduce.5.cloned.1.call-done = bf16[32,3072]{1,0:T(8,128)(2,1)} async-done(((bf16[32,3072]{1,0:T(8,128)(2,1)}), bf16[32,3072]{1,0:T(8,128)(2,1)}) %all-reduce.5.cloned.1.call-update) | async-done | bytes 196624 | tf_op jit(solution)/shard_map/psum | solution.py:192
  399.2 6.2 collective-permute-done.4
  405.5 2.5 convolution_convert_fusion.12
  409.1 7.2 fusion.22
  416.4 31.0 %all-reduce.7.cloned.1.call-done = bf16[32,3072]{1,0:T(8,128)(2,1)} async-done(((bf16[32,3072]{1,0:T(8,128)(2,1)}), bf16[32,3072]{1,0:T(8,128)(2,1)}) %all-reduce.7.cloned.1.call-update) | async-done | bytes 196624 | tf_op jit(solution)/shard_map/psum | solution.py:192
  451.7 5.6 collective-permute-done.5
  457.4 2.5 convolution_convert_fusion.11
  460.9 7.2 fusion.23
  468.3 30.9 %all-reduce.9.cloned.1.call-done = bf16[32,3072]{1,0:T(8,128)(2,1)} async-done(((bf16[32,3072]{1,0:T(8,128)(2,1)}), bf16[32,3072]{1,0:T(8,128)(2,1)}) %all-reduce.9.cloned.1.call-update) | async-done | bytes 196624 | tf_op jit(solution)/shard_map/psum | solution.py:192
  504.5 4.7 collective-permute-done.6
  509.2 2.5 convolution_convert_fusion.10
  512.8 7.3 fusion.24
  520.2 31.0 %all-reduce.11.cloned.1.call-done = bf16[32,3072]{1,0:T(8,128)(2,1)} async-done(((bf16[32,3072]{1,0:T(8,128)(2,1)}), bf16[32,3072]{1,0:T(8,128)(2,1)}) %all-reduce.11.cloned.1.call-update) | async-done | bytes 196624 | tf_op jit(solution)/shard_map/psum | solution.py:192
  555.0 6.1 collective-permute-done.7
  561.8 2.5 convolution_convert_fusion.9
  566.6 15.8 %while.12 = (s32[]{:T(128)}, bf16[4,3072,512]{2,1,0:T(8,128)(2,1)}, s32[4]{0:T(128)S(1)}, bf16[128,3072]{1,0:T(8,128)(2,1)S(1)}, bf16[128,3072]{1,0:T(8,128)(2,1...) while((s32[]{:T(128)}, bf16[4,3072,512]{2,1,0:T(8,128)(2,1)}, ...), condition=%wide.region_42.43_spmd, body=%wide.region_41.42_spmd.sunk | while | flops 403046400 | bytes 7996187 | solution.py:222
  567.9 2.7 bitcast_dynamic-update-slice_fusion.2
  571.8 2.7 bitcast_dynamic-update-slice_fusion.2
  575.8 2.7 bitcast_dynamic-update-slice_fusion.2
  579.7 2.7 bitcast_dynamic-update-slice_fusion.2
  582.4 211.3 %reduce-scatter.2.cloned.1.call-done = bf16[3072,512]{1,0:T(8,128)(2,1)} async-done(((bf16[12288,512]{1,0:T(8,128)(2,1)}), bf16[3072,512]{1,0:T(8,128)(2,1)}) %reduce-scatter.2.cloned.1.call-update) | async-done | bytes 3145744 | tf_op jit(solution)/shard_map/reduce_scatter | solution.py:225
  793.7 16.1 %fusion.25 = (f32[1,3072,512]{2,1,0:T(8,128)}, f32[1,3072,512]{2,1,0:T(8,128)}, f32[1,3072,512]{2,1,0:T(8,128)}) fusion(bf16[3072,512]{1,0:T(8,128)(2,1)} %reduce-scatter.2.cloned.1.call-done, f32[1,3072,512]{2,1,0:T(8,128)} %param.15, f32[1,3072,512]{2,1,0:T(8,128)} %param.14, f32[1,3072,512]{2,1,0:T(8,128)} %param.13), kind=kLoop, calls=%fused_computation.39 | loop fusion | flops 25165824 | bytes 40894464 | tf_op jit(solution)/shard_map/broadcast_in_dim | solution.py:234
  (284 shorter events, 43.7 us)
Async XLA Ops:
  7.2 226.1 %all-gather.6.cloned.1.call-start = ((), (), s32[]{:S(2)}) async-start(), calls=%async_computation.1 | async-start | bytes 15728640 | tf_op jit(solution)/shard_map/all_gather | solution.py:147
  12.1 13.5 %copy-start.1 = (f32[1,3072]{1,0:T(1,128)S(1)}, f32[1,3072]{1,0:T(1,128)}, u32[]{:S(2)}) copy-start(f32[1,3072]{1,0:T(1,128)} %param.12) | copy-start | bytes 36868
  12.2 383.4 %all-reduce.5.cloned.1.call-start = ((), (), s32[]{:S(2)}) async-start(), calls=%async_computation.2 | async-start | bytes 393216 | tf_op jit(solution)/shard_map/psum | solution.py:192
  242.0 18.0 %copy-start.7 = (bf16[8,16,768]{2,1,0:T(8,128)(2,1)S(1)}, bf16[8,16,768]{2,1,0:T(8,128)(2,1)}, u32[]{:S(2)}) copy-start(bf16[8,16,768]{2,1,0:T(8,128)(2,1)} %param.11) | copy-start | bytes 589828
  243.7 30.6 %copy-start.9 = (bf16[2,16,1,4,128]{4,3,1,0,2:T(4,128)(2,1)}, bf16[2,16,1,4,128]{4,3,1,0,2:T(4,128)(2,1)S(1)}, u32[]{:S(2)}) copy-start(bf16[2,16,1,4,128]{4,3,1,0,2:T(4,128)(2,1)S(1)} %get-tuple-element.137) | copy-start | bytes 98308
  243.8 30.6 %copy-start.15 = (bf16[2,16,1,4,128]{4,3,1,0,2:T(4,128)(2,1)}, bf16[2,16,1,4,128]{4,3,1,0,2:T(4,128)(2,1)S(1)}, u32[]{:S(2)}) copy-start(bf16[2,16,1,4,128]{4,3,1,0,2:T(4,128)(2,1)S(1)} %get-tuple-element.135) | copy-start | bytes 98308
  243.8 30.6 %copy-start.17 = (bf16[2,16,1,4,128]{4,3,1,0,2:T(4,128)(2,1)}, bf16[2,16,1,4,128]{4,3,1,0,2:T(4,128)(2,1)S(1)}, u32[]{:S(2)}) copy-start(bf16[2,16,1,4,128]{4,3,1,0,2:T(4,128)(2,1)S(1)} %get-tuple-element.136) | copy-start | bytes 98308
  244.6 24.1 %copy-start.38 = (f32[2,4,16]{2,1,0:T(4,128)}, f32[2,4,16]{2,1,0:T(4,128)S(1)}, u32[]{:S(2)}) copy-start(f32[2,4,16]{2,1,0:T(4,128)S(1)} %get-tuple-element.140) | copy-start | bytes 1540
  256.6 11.9 %collective-permute-start = (bf16[32,3072]{1,0:T(8,128)(2,1)S(1)}, bf16[32,3072]{1,0:T(8,128)(2,1)S(1)}, u32[]{:S(2)}, u32[]{:S(2)}) collective-permute-start(bf16[32,3072]{1,0:T(8,128)(2,1)S(1)} %fusion.133), channel_id=1, source_target_pairs={{0,16},{1,17},{2,18},{3,19},{4,20},{5,21},{6,22},{7,23},{8,24},{9,... | collective-permute-start | bytes 589832 | tf_op jit(solution)/shard_map/ppermute | solution.py:21
  275.3 19.8 %copy-start.40 = (f32[2,4,16]{2,1,0:T(4,128)}, f32[2,4,16]{2,1,0:T(4,128)S(1)}, u32[]{:S(2)}) copy-start(f32[2,4,16]{2,1,0:T(4,128)S(1)} %get-tuple-element.142) | copy-start | bytes 1540
  287.5 6.2 collective-permute-start.1
  295.1 9.7 %copy-start.29 = (f32[32]{0:T(128)}, f32[32]{0:T(128)S(1)}, u32[]{:S(2)}) copy-start(f32[32]{0:T(128)S(1)} %add_rsqrt_fusion.3) | copy-start | bytes 388
  300.7 22.4 %copy-start.23 = (bf16[2,16,1,4,128]{4,3,1,0,2:T(4,128)(2,1)}, bf16[2,16,1,4,128]{4,3,1,0,2:T(4,128)(2,1)S(1)}, u32[]{:S(2)}) copy-start(bf16[2,16,1,4,128]{4,3,1,0,2:T(4,128)(2,1)S(1)} %get-tuple-element.129) | copy-start | bytes 98308
  301.5 27.1 %copy-start.42 = (f32[2,4,16]{2,1,0:T(4,128)}, f32[2,4,16]{2,1,0:T(4,128)S(1)}, u32[]{:S(2)}) copy-start(f32[2,4,16]{2,1,0:T(4,128)S(1)} %get-tuple-element.144) | copy-start | bytes 1540
  301.8 21.2 %copy-start.3 = (bf16[2,16,4,128]{3,2,1,0:T(4,128)(2,1)}, bf16[2,16,4,128]{3,2,1,0:T(4,128)(2,1)S(1)}, u32[]{:S(2)}) copy-start(bf16[2,16,4,128]{3,2,1,0:T(4,128)(2,1)S(1)} %copy.131) | copy-start | bytes 98308
  313.6 9.0 %collective-permute-start.2 = (bf16[32,3072]{1,0:T(8,128)(2,1)S(1)}, bf16[32,3072]{1,0:T(8,128)(2,1)S(1)}, u32[]{:S(2)}, u32[]{:S(2)}) collective-permute-start(bf16[32,3072]{1,0:T(8,128)(2,1)S(1)} %fusion.128), channel_id=1, source_target_pairs={{0,16},{1,17},{2,18},{3,19},{4,20},{5,21},{6,22},{7,23},{8,24},{9,... | collective-permute-start | bytes 589832 | tf_op jit(solution)/shard_map/ppermute | solution.py:21
  328.6 19.9 %copy-start.4 = (bf16[2,16,4,128]{3,2,1,0:T(4,128)(2,1)S(1)}, bf16[2,16,4,128]{3,2,1,0:T(4,128)(2,1)}, u32[]{:S(2)}) copy-start(bf16[2,16,4,128]{3,2,1,0:T(4,128)(2,1)} %copy-done.3) | copy-start | bytes 98308
  328.7 22.2 %copy-start.27 = (bf16[2,16,1,4,128]{4,3,1,0,2:T(4,128)(2,1)}, bf16[2,16,1,4,128]{4,3,1,0,2:T(4,128)(2,1)S(1)}, u32[]{:S(2)}) copy-start(bf16[2,16,1,4,128]{4,3,1,0,2:T(4,128)(2,1)S(1)} %get-tuple-element.127) | copy-start | bytes 98308
  341.5 9.0 %collective-permute-start.3 = (bf16[32,3072]{1,0:T(8,128)(2,1)S(1)}, bf16[32,3072]{1,0:T(8,128)(2,1)S(1)}, u32[]{:S(2)}, u32[]{:S(2)}) collective-permute-start(bf16[32,3072]{1,0:T(8,128)(2,1)S(1)} %fusion.129), channel_id=1, source_target_pairs={{0,16},{1,17},{2,18},{3,19},{4,20},{5,21},{6,22},{7,23},{8,24},{9,... | collective-permute-start | bytes 589832 | tf_op jit(solution)/shard_map/ppermute | solution.py:21
  364.8 43.4 %copy-start.37 = (f32[2,4,16,16]{2,3,1,0:T(8,128)S(1)}, f32[2,4,16,16]{2,3,1,0:T(8,128)}, u32[]{:S(2)}) copy-start(f32[2,4,16,16]{2,3,1,0:T(8,128)} %get-tuple-element.147) | copy-start | bytes 24580
  364.8 43.4 %copy-start.45 = (f32[2,4,16]{2,1,0:T(4,128)S(1)}, f32[2,4,16]{2,1,0:T(4,128)}, u32[]{:S(2)}) copy-start(f32[2,4,16]{2,1,0:T(4,128)} %copy-done.44) | copy-start | bytes 1540
  364.8 43.6 %copy-start.28 = (bf16[2,16,1,4,128]{4,3,1,0,2:T(4,128)(2,1)S(1)}, bf16[2,16,1,4,128]{4,3,1,0,2:T(4,128)(2,1)}, u32[]{:S(2)}) copy-start(bf16[2,16,1,4,128]{4,3,1,0,2:T(4,128)(2,1)} %copy-done.27) | copy-start | bytes 98308
  364.8 82.6 %all-reduce.7.cloned.1.call-start = ((), (), s32[]{:S(2)}) async-start(), calls=%async_computation.3 | async-start | bytes 393216 | tf_op jit(solution)/shard_map/psum | solution.py:192
  397.9 7.6 collective-permute-start.4
  409.0 38.4 %copy-start.32 = (f32[32]{0:T(128)S(1)}, f32[32]{0:T(128)}, u32[]{:S(2)}) copy-start(f32[32]{0:T(128)} %copy-done.31) | copy-start | bytes 388
  409.0 50.9 %copy-start.14 = (bf16[2,16,1,4,128]{4,3,1,0,2:T(4,128)(2,1)S(1)}, bf16[2,16,1,4,128]{4,3,1,0,2:T(4,128)(2,1)}, u32[]{:S(2)}) copy-start(bf16[2,16,1,4,128]{4,3,1,0,2:T(4,128)(2,1)} %copy-done.13) | copy-start | bytes 98308
  409.0 51.0 %copy-start.24 = (bf16[2,16,1,4,128]{4,3,1,0,2:T(4,128)(2,1)S(1)}, bf16[2,16,1,4,128]{4,3,1,0,2:T(4,128)(2,1)}, u32[]{:S(2)}) copy-start(bf16[2,16,1,4,128]{4,3,1,0,2:T(4,128)(2,1)} %copy-done.23) | copy-start | bytes 98308
  409.0 51.0 %copy-start.36 = (f32[2,4,16,16]{2,3,1,0:T(8,128)S(1)}, f32[2,4,16,16]{2,3,1,0:T(8,128)}, u32[]{:S(2)}) copy-start(f32[2,4,16,16]{2,3,1,0:T(8,128)} %get-tuple-element.145) | copy-start | bytes 24580
  409.0 51.0 %copy-start.43 = (f32[2,4,16]{2,1,0:T(4,128)S(1)}, f32[2,4,16]{2,1,0:T(4,128)}, u32[]{:S(2)}) copy-start(f32[2,4,16]{2,1,0:T(4,128)} %copy-done.42) | copy-start | bytes 1540
  416.3 44.0 %copy-start.26 = (bf16[2,16,1,4,128]{4,3,1,0,2:T(4,128)(2,1)S(1)}, bf16[2,16,1,4,128]{4,3,1,0,2:T(4,128)(2,1)}, u32[]{:S(2)}) copy-start(bf16[2,16,1,4,128]{4,3,1,0,2:T(4,128)(2,1)} %copy-done.25) | copy-start | bytes 98308
  416.3 82.9 %all-reduce.9.cloned.1.call-start = ((), (), s32[]{:S(2)}) async-start(), calls=%async_computation.4 | async-start | bytes 393216 | tf_op jit(solution)/shard_map/psum | solution.py:192
  449.8 7.6 collective-permute-start.5
  460.9 38.3 %copy-start.30 = (f32[32]{0:T(128)S(1)}, f32[32]{0:T(128)}, u32[]{:S(2)}) copy-start(f32[32]{0:T(128)} %copy-done.29) | copy-start | bytes 388
  468.1 43.6 %copy-start.12 = (bf16[2,16,1,4,128]{4,3,1,0,2:T(4,128)(2,1)S(1)}, bf16[2,16,1,4,128]{4,3,1,0,2:T(4,128)(2,1)}, u32[]{:S(2)}) copy-start(bf16[2,16,1,4,128]{4,3,1,0,2:T(4,128)(2,1)} %copy-done.11) | copy-start | bytes 98308
  468.1 43.8 %copy-start.20 = (bf16[2,16,1,4,128]{4,3,1,0,2:T(4,128)(2,1)S(1)}, bf16[2,16,1,4,128]{4,3,1,0,2:T(4,128)(2,1)}, u32[]{:S(2)}) copy-start(bf16[2,16,1,4,128]{4,3,1,0,2:T(4,128)(2,1)} %copy-done.19) | copy-start | bytes 98308
  468.1 43.8 %copy-start.35 = (f32[2,4,16,16]{2,3,1,0:T(8,128)S(1)}, f32[2,4,16,16]{2,3,1,0:T(8,128)}, u32[]{:S(2)}) copy-start(f32[2,4,16,16]{2,3,1,0:T(8,128)} %get-tuple-element.143) | copy-start | bytes 24580
  468.1 43.8 %copy-start.41 = (f32[2,4,16]{2,1,0:T(4,128)S(1)}, f32[2,4,16]{2,1,0:T(4,128)}, u32[]{:S(2)}) copy-start(f32[2,4,16]{2,1,0:T(4,128)} %copy-done.40) | copy-start | bytes 1540
  468.1 44.0 %copy-start.22 = (bf16[2,16,1,4,128]{4,3,1,0,2:T(4,128)(2,1)S(1)}, bf16[2,16,1,4,128]{4,3,1,0,2:T(4,128)(2,1)}, u32[]{:S(2)}) copy-start(bf16[2,16,1,4,128]{4,3,1,0,2:T(4,128)(2,1)} %copy-done.21) | copy-start | bytes 98308
  468.2 83.0 %all-reduce.11.cloned.1.call-start = ((), (), s32[]{:S(2)}) async-start(), calls=%async_computation.5 | async-start | bytes 393216 | tf_op jit(solution)/shard_map/psum | solution.py:192
  501.6 7.6 collective-permute-start.6
  512.8 7.4 copy-start.2
  520.1 44.3 %copy-start.10 = (bf16[2,16,1,4,128]{4,3,1,0,2:T(4,128)(2,1)S(1)}, bf16[2,16,1,4,128]{4,3,1,0,2:T(4,128)(2,1)}, u32[]{:S(2)}) copy-start(bf16[2,16,1,4,128]{4,3,1,0,2:T(4,128)(2,1)} %copy-done.9) | copy-start | bytes 98308
  520.1 44.4 %copy-start.16 = (bf16[2,16,1,4,128]{4,3,1,0,2:T(4,128)(2,1)S(1)}, bf16[2,16,1,4,128]{4,3,1,0,2:T(4,128)(2,1)}, u32[]{:S(2)}) copy-start(bf16[2,16,1,4,128]{4,3,1,0,2:T(4,128)(2,1)} %copy-done.15) | copy-start | bytes 98308
  520.1 44.4 %copy-start.34 = (f32[2,4,16,16]{2,3,1,0:T(8,128)S(1)}, f32[2,4,16,16]{2,3,1,0:T(8,128)}, u32[]{:S(2)}) copy-start(f32[2,4,16,16]{2,3,1,0:T(8,128)} %get-tuple-element.141) | copy-start | bytes 24580
  520.1 44.4 %copy-start.39 = (f32[2,4,16]{2,1,0:T(4,128)S(1)}, f32[2,4,16]{2,1,0:T(4,128)}, u32[]{:S(2)}) copy-start(f32[2,4,16]{2,1,0:T(4,128)} %copy-done.38) | copy-start | bytes 1540
  520.1 44.6 %copy-start.18 = (bf16[2,16,1,4,128]{4,3,1,0,2:T(4,128)(2,1)S(1)}, bf16[2,16,1,4,128]{4,3,1,0,2:T(4,128)(2,1)}, u32[]{:S(2)}) copy-start(bf16[2,16,1,4,128]{4,3,1,0,2:T(4,128)(2,1)} %copy-done.17) | copy-start | bytes 98308
  520.1 273.6 %reduce-scatter.2.cloned.1.call-start = ((), (), s32[]{:S(2)}) async-start(), calls=%async_computation.6 | async-start | bytes 15728640 | tf_op jit(solution)/shard_map/reduce_scatter | solution.py:225
  553.5 7.6 collective-permute-start.7
  (12 other events, 32.9 us)
Sparse Core Ops, SparseCore 0:
  12.3 220.9 all-gather.5
  365.0 30.5 all-reduce.4
  416.4 30.9 all-reduce.6
  468.3 30.9 all-reduce.8
  520.2 30.9 all-reduce.10
  582.5 211.1 reduce-scatter.1
